TPU v7x, 128 devices: a whole 4x4x4 slice. The times are simulated.
128 devices in a mesh: dp: 16 (over x, z_hi, core), mp: 8 (over y, z_lo).
Axes of the slice: x: 4, y: 4, z: 4 (z_hi: 2, z_lo: 2; z = z_hi * 2 + z_lo), core: 2. Of those that a mesh axis runs over, the one named last changes fastest.
Arguments:
- adapter_inputs: bfloat16 [49152, 64], P('dp'), may hold values from -6 to 6
- out_grads: bfloat16 [49152, 8192], P('dp', 'mp'), may hold values from -6 to 6
- routes: int32 [49152], P('dp'), may hold values from 0 to 1
- input_eigen_basis: float32 [2, 64, 64], replicated, may hold values from -0.75 to 0.75
- output_eigen_basis: bfloat16 [8192, 8192], P(None, 'mp'), may hold values from -0.0625 to 0.0625
- eigen_values: float32 [2, 64, 8192], P(None, None, 'mp'), may hold values from 0.05 to 1
- query_grads: bfloat16 [96, 2, 64, 8192], P('dp', None, None, 'mp'), may hold values from -6 to 6
Outputs:
- scores: float32 [48, 96], P('dp')
All inputs are finite; a program needn't handle non-finite values.
Results may differ from a plain program's by a relative error of at most 0.0048.
Values may be sent and summed in bfloat16 or wider, within the bound.
A program may use at most 256 MiB of HBM per device.

v0:
```python
import jax
import jax.numpy as jnp
from jax import lax
from jax.sharding import PartitionSpec as P

LEN = 1024


damping = 0.1


def local(
    adapter_inputs,
    out_grads,
    routes,
    input_eigen_basis,
    output_eigen_basis,
    eigen_values,
    query_grads,
):
    tokens = adapter_inputs.shape[0]
    experts = input_eigen_basis.shape[0]
    rank = input_eigen_basis.shape[1]
    local_width = out_grads.shape[1]
    width = output_eigen_basis.shape[0]
    seqs = tokens // LEN
    spread = jnp.einsum(
        "tr,ers->tes",
        adapter_inputs.astype(jnp.float32),
        input_eigen_basis,
        precision=lax.Precision.HIGHEST,
    )
    picked_option = routes[:, None] == jnp.arange(experts, dtype=jnp.int32)[None, :]
    input_rotated_rows = jnp.where(picked_option[:, :, None], spread, 0.0).astype(jnp.bfloat16)
    input_rotated_rows = input_rotated_rows.reshape(seqs, LEN, experts * rank)
    sequence_gradients = out_grads.reshape(seqs, LEN, local_width)
    unrotated_gradients = jnp.einsum(
        "tnh,tnj->thj", input_rotated_rows, sequence_gradients, preferred_element_type=jnp.float32
    ).astype(jnp.bfloat16)
    rotated = jnp.einsum(
        "skd,dc->skc",
        lax.all_gather(unrotated_gradients, "mp", axis=2, tiled=True),
        output_eigen_basis,
        preferred_element_type=jnp.float32,
    )
    training_gradients = rotated.astype(jnp.bfloat16)
    shifted = eigen_values + damping
    scale = 1.0 / jnp.sqrt(jnp.float32(LEN * experts * rank * width))
    train_flat = training_gradients.reshape(seqs, -1).astype(jnp.float32)
    piece = lax.all_gather(query_grads, "dp", axis=0, tiled=True)
    precond = (piece.astype(jnp.float32) / shifted[None]).reshape(piece.shape[0], -1)
    part = jnp.dot(train_flat, precond.T, precision=lax.Precision.HIGHEST)
    totals = lax.psum(part, "mp")
    return totals * scale


def solution(mesh):
    placed = (
        P("dp", None),
        P("dp", "mp"),
        P("dp"),
        P(),
        P(None, "mp"),
        P(None, None, "mp"),
        P("dp", None, None, "mp"),
    )
    return jax.shard_map(
        local, mesh=mesh, in_specs=placed, out_specs=P("dp", None), check_vma=False
    )
```

profile of v0, /device:TPU:0, one launch (start us, length us, event | category | flops | bytes accessed | tf_op | source)
XLA Modules:
  0.0 426.4 jit_solution(9849895581080400399)
XLA Ops:
  6.5 0.0 copy-start
  6.5 0.0 all-gather.3.cloned.1.call-start
  6.5 1.0 copy.10
  7.5 0.7 iota_compare_fusion
  8.2 0.0 copy-done
  8.3 0.8 fusion.9
  9.0 0.1 select_convert_fusion
  9.2 0.0 copy-start.2
  9.2 1.2 reshape.34
  10.3 5.0 %convolution_convert_fusion = bf16[3,128,1024]{2,1,0:T(8,128)(2,1)} fusion(bf16[3,1024,1024]{2,1,0:T(8,128)(2,1)} %bitcast.30, bf16[3,1024,128]{1,0,2:T(4,128)(2,1)S(1)} %reshape.34), kind=kOutput, calls=%fused_computation.5 | convolution fusion | flops 805699584 | bytes 7864320 | tf_op jit(solution)/shard_map/tnh,tnj->thj/dot_general | solution.py:37
  15.3 0.0 all-gather.3.cloned.1.call-update
  15.4 0.2 all-gather.5.cloned.1.call-start
  15.6 0.5 all-gather.5.cloned.1.call-update
  16.1 0.0 copy-done.2
  16.1 0.1 broadcast_add_fusion
  16.2 130.9 %all-gather.3.cloned.1.call-done = bf16[3,128,8192]{2,1,0:T(8,128)(2,1)} async-done(((bf16[3,128,1024]{2,1,0:T(8,128)(2,1)}), bf16[3,128,8192]{2,1,0:T(8,128)(2,1)}) %all-gather.3.cloned.1.call-update) | async-done | bytes 6291472 | tf_op jit(solution)/shard_map/all_gather | solution.py:42
  147.1 12.2 %fusion.5 = bf16[1,3,128,1024]{3,2,1,0:T(8,128)(2,1)S(1)} fusion(bf16[3,128,8192]{2,1,0:T(8,128)(2,1)} %all-gather.3.cloned.1.call-done, bf16[8192,1024]{1,0:T(8,128)(2,1)} %param.11), kind=kOutput, calls=%fused_computation.6 | convolution fusion | flops 6442844160 | bytes 23855104 | tf_op jit(solution)/shard_map/skd,dc->skc/dot_general | solution.py:40
  159.2 0.7 copy.12
  159.9 140.0 %all-gather.5.cloned.1.call-done = bf16[96,2,64,1024]{3,2,1,0:T(8,128)(2,1)} async-done(((bf16[6,2,64,1024]{3,2,1,0:T(8,128)(2,1)}), bf16[96,2,64,1024]{3,2,1,0:T(8,128)(2,1)}) %all-gather.5.cloned.1.call-update) | async-done | bytes 25165840 | tf_op jit(solution)/shard_map/all_gather | solution.py:50
  299.9 27.2 %convert_divide_fusion = f32[96,2,64,1024]{3,2,1,0:T(8,128)} fusion(bf16[96,2,64,1024]{3,2,1,0:T(8,128)(2,1)} %all-gather.5.cloned.1.call-done, f32[2,64,1024]{2,1,0:T(8,128)S(1)} %broadcast_add_fusion), kind=kLoop, calls=%fused_computation | loop fusion | flops 25165824 | bytes 76021760 | tf_op jit(solution)/shard_map/div | solution.py:51
  327.1 45.8 %copy.13 = f32[12,8,128,1024]{3,1,2,0:T(8,128)} copy(f32[12,8,128,1024]{3,2,1,0:T(8,128)} %bitcast.27) | data formatting | bytes 100663296
  372.9 0.0 copy-start.1
  372.9 27.2 %fusion.10 = f32[3,96]{1,0:T(4,128)S(1)} fusion(bf16[3,131072]{1,0:T(4,128)(2,1)S(1)} %bitcast.28, f32[96,131072]{1,0:T(8,128)} %bitcast.26), kind=kOutput, calls=%fused_computation.12 | convolution fusion | flops 452984832 | bytes 51119232 | tf_op jit(solution)/shard_map/dot_general | solution.py:52
  400.2 18.8 %psum.7 = f32[3,96]{1,0:T(4,128)S(1)} all-reduce(f32[3,96]{1,0:T(4,128)S(1)} %fusion.10), channel_id=1, replica_groups=mesh['dp'=16,'mp'=8] {'mp'}, use_global_device_ids=true, to_apply=%region_0.1 | all-reduce | flops 288 | bytes 2304 | tf_op jit(solution)/shard_map/psum | solution.py:53
  419.0 0.6 broadcast_multiply_fusion
  419.6 0.0 copy-done.1
Async XLA Ops:
  6.5 1.7 copy-start
  6.5 140.5 %all-gather.3.cloned.1.call-start = ((), (), s32[]{:S(2)}) async-start(), calls=%async_computation | async-start | bytes 7077888 | tf_op jit(solution)/shard_map/all_gather | solution.py:42
  9.2 7.0 %copy-start.2 = (f32[2,64,1024]{2,1,0:T(8,128)S(1)}, f32[2,64,1024]{2,1,0:T(8,128)}, u32[]{:S(2)}) copy-start(f32[2,64,1024]{2,1,0:T(8,128)} %param.12) | copy-start | bytes 1572868
  15.4 284.6 %all-gather.5.cloned.1.call-start = ((), (), s32[]{:S(2)}) async-start(), calls=%async_computation.1 | async-start | bytes 26738688 | tf_op jit(solution)/shard_map/all_gather | solution.py:50
  372.9 46.6 %copy-start.1 = (bf16[3072,64]{0,1:T(8,128)(2,1)S(1)}, bf16[3072,64]{0,1:T(8,128)(2,1)}, u32[]{:S(2)}) copy-start(bf16[3072,64]{0,1:T(8,128)(2,1)} %param.7) | copy-start | bytes 1179652
Sparse Core Ops, SparseCore 0:
  15.5 131.5 all-gather.2
  149.5 150.4 all-gather.4
where the time goes:
time: 427 us; the launch traced here: 426 us
  waiting for transfers between devices  271 us (63%)
  local copies, waits for them, and re-layouts  48.6 us (11%)
  matrix products  45.2 us (11%)
  other arithmetic  28.7 us (7%)
  blocking collectives  18.8 us (4%)
  between operations  13.5 us (3%)
    all_gather x1, waiting for transfers between devices, local(): piece = lax.all_gather(query_grads, 'dp', axis=0, tiled=True)  140 us
    all_gather x1, waiting for transfers between devices, local(): lax.all_gather(unrotated_gradients, 'mp', axis=2, tiled=True)  131 us
    unnamed x9, local copies, waits for them, and re-layouts  47.5 us
    dot_general x1, matrix products, local(): part = jnp.dot(train_flat, precond.T, precision=lax.Precision.HIGHEST)  27.2 us
    div x1, other arithmetic, local(): piece.astype(jnp.float32) / shifted[None]  27.2 us
    psum x1, blocking collectives, local(): totals = lax.psum(part, 'mp')  18.8 us
    dot_general x1, matrix products, local(): jnp.einsum('skd,dc->skc', lax.all_gather(unrotated_gradients, 'mp', axis=...  12.2 us
  transfers between devices with their start and end apart: 2, of which 2 were waited for; matrix products, arithmetic and copies ran while one was open for 3% of the time, Pallas kernels for 0%

commit v1 on v0

v1 whole, which is shorter than its diff:
```python
import functools
import math

import jax
import jax.numpy as jnp
from jax import lax
from jax.experimental import pallas as pl
from jax.experimental.pallas import tpu as pltpu
from jax.sharding import PartitionSpec as P

LEN = 1024
LANES = 128
DAMPING = 0.1
F32, BF16 = jnp.float32, jnp.bfloat16

GROUPS = 8
CORES = 2
YS = 4
NT = (((1,), (1,)), ((), ()))


def kernel(
    dims,
    a_ref, routes_ref, basis_ref, g_hbm, u_hbm, eig_hbm, q_hbm,
    out_ref,
    g_v, u_v, eig_v, raw, gat, qbuf, qwide, qrow, acc, part, got, mine, all_mine,
    g_sem, u_sem, l_sem,
    a_send, a_recv, z_send, z_recv, y_send, y_recv, f_send, f_recv,
    q_send, q_recv, c_send, c_recv, r_send, r_recv, t_send, t_recv,
):
    seqs, rows, rank, experts, width, queries, blk = dims
    piece = seqs * blk
    dp, mp = lax.axis_index("dp"), lax.axis_index("mp")
    s, k = dp // CORES, dp % CORES
    y, l = mp // 2, mp % 2

    def dp_peer(b):
        return {"dp": b * CORES + k, "mp": mp}

    def mp_peer(m):
        return {"dp": dp, "mp": m}

    def at(dy, dl):
        return ((y + dy) % YS) * 2 + (l + dl) % 2

    def remote(src, dst, send, recv, dev):
        return pltpu.make_async_remote_copy(
            src_ref=src, dst_ref=dst, send_sem=send, recv_sem=recv, device_id=dev
        )

    def src_of(o):
        return (s + GROUPS - o) % GROUPS

    for n in range(seqs):
        pltpu.make_async_copy(g_hbm.at[n], g_v.at[n], g_sem.at[n]).start()
    eig_copy = pltpu.make_async_copy(
        eig_hbm.at[pl.ds(pl.multiple_of(s * blk, blk), blk), :], eig_v, l_sem.at[0]
    )
    eig_copy.start()

    barrier = pltpu.get_barrier_semaphore()
    for o in range(1, GROUPS):
        pl.semaphore_signal(barrier, inc=1, device_id=dp_peer((s + o) % GROUPS))
        pl.semaphore_signal(barrier, inc=1, device_id=mp_peer((mp + o) % GROUPS))
    partner = {"dp": s * CORES + 1 - k, "mp": mp}
    pl.semaphore_signal(barrier, inc=1, device_id=partner)

    for m in range(GROUPS):
        pltpu.make_async_copy(u_hbm.at[m], u_v.at[m], u_sem.at[m]).start()

    basis = basis_ref[...]
    parts, rest = [], basis
    for _ in range(3):
        parts.append(rest.astype(BF16))
        rest = rest - parts[-1].astype(F32)
    row_expert = lax.broadcasted_iota(jnp.int32, (rows, 1), 0) // rank

    def sequence(n, carry):
        pltpu.make_async_copy(g_hbm.at[n], g_v.at[n], g_sem.at[n]).wait()
        a = a_ref[n]
        spread = lax.dot_general(parts[2], a, NT, preferred_element_type=F32)
        spread += lax.dot_general(parts[1], a, NT, preferred_element_type=F32)
        spread += lax.dot_general(parts[0], a, NT, preferred_element_type=F32)
        rotated = jnp.where(routes_ref[n] == row_expert, spread, 0.0).astype(BF16)
        sums = jnp.dot(rotated, g_v[n], preferred_element_type=F32).astype(BF16)
        raw[:, pl.ds(pl.multiple_of(n * blk, blk), blk), :] = sums.reshape(GROUPS, blk, width)
        return carry

    lax.fori_loop(0, seqs, sequence, 0)
    gat[mp, s] = raw[s]

    pl.semaphore_wait(barrier, 2 * (GROUPS - 1) + 1)

    def a_copy(o):
        b = (s + o) % GROUPS
        return remote(raw.at[b], gat.at[mp, s], a_send.at[o], a_recv.at[o], dp_peer(b))

    def y_copy(o, side, way):
        slot = gat.at[at(0, side), src_of(o)]
        return remote(
            slot, slot, y_send.at[side, way, o], y_recv.at[side, way, o],
            mp_peer(at(1 if way == 0 else YS - 1, 0)),
        )

    def y_landed(o, side, way):
        slot = gat.at[at(YS - 1 if way == 0 else 1, side), src_of(o)]
        return remote(
            slot, slot, y_send.at[side, way, o], y_recv.at[side, way, o],
            mp_peer(at(1 if way == 0 else YS - 1, 0)),
        )

    def f_copy(o, side, way):
        slot = gat.at[at(YS - 1 if way == 0 else 1, side), src_of(o)]
        return remote(
            slot, slot, f_send.at[side, o], f_recv.at[side, o],
            mp_peer(at(1 if way == 0 else YS - 1, 0)),
        )

    def f_landed(o, side):
        slot = gat.at[at(2, side), src_of(o)]
        return remote(slot, slot, f_send.at[side, o], f_recv.at[side, o], mp_peer(at(1, 0)))

    def z_copy(o):
        slot = gat.at[mp, src_of(o)]
        return remote(slot, slot, z_send.at[o], z_recv.at[o], mp_peer(at(0, 1)))

    def z_landed(o):
        slot = gat.at[at(0, 1), src_of(o)]
        return remote(slot, slot, z_send.at[o], z_recv.at[o], mp_peer(at(0, 1)))

    def a_landed(o):
        slot = gat.at[mp, src_of(o)]
        return remote(slot, slot, a_send.at[o], a_recv.at[o], dp_peer(src_of(o)))

    def q_source(b):
        return q_hbm.at[:, pl.ds(pl.multiple_of(b * blk, blk), blk), :]

    def q_copy(o):
        b = (s + o) % GROUPS
        return remote(q_source(b), qbuf.at[s, k], q_send.at[o], q_recv.at[o], dp_peer(b))

    def q_landed(o):
        slot = qbuf.at[src_of(o), k]
        return remote(slot, slot, q_send.at[o], q_recv.at[o], dp_peer(src_of(o)))

    def send_own(o):
        z_copy(o).start()
        y_copy(o, 0, 0).start()
        y_copy(o, 0, 1).start()

    def each(low, high, body):
        def run(o, carry):
            body(o)
            return carry

        lax.fori_loop(low, high, run, 0)

    each(1, GROUPS, lambda o: a_copy(o).start())
    send_own(0)

    def arrived(o):
        a_landed(o).wait_recv()
        send_own(o)

    each(1, GROUPS, arrived)

    q_own = pltpu.make_async_copy(q_source(s), qbuf.at[s, k], l_sem.at[1])
    q_own.start()
    each(1, GROUPS, lambda o: q_copy(o).start())

    def multiply(m, first):
        pltpu.make_async_copy(u_hbm.at[m], u_v.at[m], u_sem.at[m]).wait()
        step = 256

        def column(i, carry):
            cols = pl.ds(pl.multiple_of(i * step, step), step)
            product = jnp.dot(
                gat[m].reshape(GROUPS * piece, width), u_v[m, :, cols],
                preferred_element_type=F32,
            )
            for half in range(step // LANES):
                lanes = i * (step // LANES) + half
                term = product[:, half * LANES : (half + 1) * LANES]
                acc[lanes] = term if first else acc[lanes] + term
            return carry

        lax.fori_loop(0, width // step, column, 0)

    multiply(mp, True)

    def forward_even(o, side):
        y_landed(o, side, 0).wait_recv()
        f_copy(o, side, 0).start()

    def forward_odd(o, side):
        y_landed(o, side, 1).wait_recv()
        f_copy(o, side, 1).start()

    def pair(i):
        for o in (2 * i, 2 * i + 1):
            z_landed(o).wait_recv()
            y_copy(o, 1, 0).start()
            y_copy(o, 1, 1).start()
        forward_even(2 * i, 0)
        forward_odd(2 * i + 1, 0)

    each(0, GROUPS // 2, pair)
    multiply(at(0, 1), False)

    def rest_of(side):
        def body(i):
            y_landed(2 * i, side, 1).wait_recv()
            y_landed(2 * i + 1, side, 0).wait_recv()
        return body

    each(0, GROUPS // 2, rest_of(0))
    multiply(at(1, 0), False)
    multiply(at(YS - 1, 0), False)

    each(1, GROUPS, lambda o: q_landed(o).wait_recv())
    q_own.wait()
    c_copy = remote(qbuf.at[:, k], qbuf.at[:, k], c_send.at[0], c_recv.at[0], partner)
    c_copy.start()

    def pair_far(i):
        forward_even(2 * i, 1)
        forward_odd(2 * i + 1, 1)

    each(0, GROUPS // 2, pair_far)

    remote(qbuf.at[:, 1 - k], qbuf.at[:, 1 - k], c_send.at[0], c_recv.at[0], partner).wait_recv()
    total = GROUPS * CORES * queries

    def widen(i, carry):
        chunk = queries * CORES * blk
        own = pl.ds(pl.multiple_of(i * chunk, chunk), chunk)
        for lanes in range(width // LANES):
            cols = qbuf[i, :, :, :, lanes * LANES : (lanes + 1) * LANES]
            qwide[lanes, own, :] = cols.reshape(chunk, LANES).astype(F32)
        return carry

    lax.fori_loop(0, GROUPS, widen, 0)

    def regroup(r, carry):
        for lanes in range(width // LANES):
            cols = qwide[lanes, pl.ds(r, total, stride=blk), :]
            qrow[r, :, lanes * LANES : (lanes + 1) * LANES] = cols.astype(BF16)
        return carry

    lax.fori_loop(0, blk, regroup, 0)
    eig_copy.wait()
    eig_v[...] = 1.0 / (eig_v[...] + DAMPING)

    each(0, GROUPS, lambda o: f_landed(o, 0).wait_recv())
    multiply(at(2, 0), False)
    each(0, GROUPS // 2, rest_of(1))
    multiply(at(1, 1), False)
    multiply(at(YS - 1, 1), False)
    each(0, GROUPS, lambda o: f_landed(o, 1).wait_recv())
    multiply(at(2, 1), False)

    count = GROUPS * seqs

    def score(r, carry):
        train = jnp.concatenate(
            [acc[lanes, pl.ds(r, count, stride=blk), :] for lanes in range(width // LANES)], axis=1
        )
        train = train.astype(BF16).astype(F32)
        train = train * eig_v[pl.ds(r, 1), :]
        high = train.astype(BF16)
        low = (train - high.astype(F32)).astype(BF16)
        carry += lax.dot_general(high, qrow[r], NT, preferred_element_type=F32)
        carry += lax.dot_general(low, qrow[r], NT, preferred_element_type=F32)
        return carry

    scores = lax.fori_loop(0, blk, score, jnp.zeros((count, total), F32))
    part[...] = jnp.zeros(part.shape, F32)
    for b in range(GROUPS):
        part[b, :seqs, :total] = scores[b * seqs : (b + 1) * seqs]

    def r_copy(o):
        b = (s + o) % GROUPS
        return remote(part.at[b], got.at[s], r_send.at[o], r_recv.at[o], dp_peer(b))

    def r_landed(o):
        slot = got.at[src_of(o)]
        return remote(slot, slot, r_send.at[o], r_recv.at[o], dp_peer(src_of(o)))

    each(1, GROUPS, lambda o: r_copy(o).start())
    got[s] = part[s]
    each(1, GROUPS, lambda o: r_landed(o).wait_recv())
    mine[...] = jnp.sum(got[...], axis=0)

    def t_copy(o):
        m = (mp + o) % GROUPS
        return remote(mine, all_mine.at[mp], t_send.at[o], t_recv.at[o], mp_peer(m))

    def t_landed(o):
        m = (mp + GROUPS - o) % GROUPS
        slot = all_mine.at[m]
        return remote(slot, slot, t_send.at[o], t_recv.at[o], mp_peer(m))

    each(1, GROUPS, lambda o: t_copy(o).start())
    all_mine[mp] = mine[...]
    each(1, GROUPS, lambda o: t_landed(o).wait_recv())
    result = jnp.sum(all_mine[...], axis=0)
    scale = 1.0 / math.sqrt(LEN * rows * width * GROUPS)
    out_ref[...] = result[:seqs, :total] * scale

    def sent(o):
        a_copy(o).wait_send()
        q_copy(o).wait_send()
        r_copy(o).wait_send()
        t_copy(o).wait_send()

    each(1, GROUPS, sent)

    def sent_pieces(o):
        z_copy(o).wait_send()
        for side in (0, 1):
            y_copy(o, side, 0).wait_send()
            y_copy(o, side, 1).wait_send()

    each(0, GROUPS, sent_pieces)

    def sent_forward(i):
        for side in (0, 1):
            f_copy(2 * i, side, 0).wait_send()
            f_copy(2 * i + 1, side, 1).wait_send()

    each(0, GROUPS // 2, sent_forward)
    c_copy.wait_send()


def local(adapter_inputs, out_grads, routes, input_eigen_basis, output_eigen_basis, eigen_values, query_grads):
    tokens, rank = adapter_inputs.shape
    experts = input_eigen_basis.shape[0]
    rows = experts * rank
    width = out_grads.shape[1]
    queries = query_grads.shape[0]
    seqs = tokens // LEN
    blk = rows // GROUPS
    dims = (seqs, rows, rank, experts, width, queries, blk)
    piece = seqs * blk
    total = GROUPS * CORES * queries
    vmem, hbm = pl.BlockSpec(memory_space=pltpu.VMEM), pl.BlockSpec(memory_space=pl.ANY)
    dma = pltpu.SemaphoreType.DMA
    return pl.pallas_call(
        functools.partial(kernel, dims),
        out_shape=jax.ShapeDtypeStruct((seqs, total), F32),
        in_specs=[vmem, vmem, vmem, hbm, hbm, hbm, hbm],
        out_specs=vmem,
        scratch_shapes=[
            pltpu.VMEM((seqs, LEN, width), BF16),
            pltpu.VMEM((GROUPS, width, width), BF16),
            pltpu.VMEM((blk, width), F32),
            pltpu.VMEM((GROUPS, piece, width), BF16),
            pltpu.VMEM((GROUPS, GROUPS, piece, width), BF16),
            pltpu.VMEM((GROUPS, CORES, queries, blk, width), BF16),
            pltpu.VMEM((width // LANES, total * blk, LANES), F32),
            pltpu.VMEM((blk, total, width), BF16),
            pltpu.VMEM((width // LANES, GROUPS * piece, LANES), F32),
            pltpu.VMEM((GROUPS, 8, 128), F32),
            pltpu.VMEM((GROUPS, 8, 128), F32),
            pltpu.VMEM((8, 128), F32),
            pltpu.VMEM((GROUPS, 8, 128), F32),
            dma((seqs,)), dma((GROUPS,)), dma((2,)),
            dma((GROUPS,)), dma((GROUPS,)), dma((GROUPS,)), dma((GROUPS,)),
            dma((2, 2, GROUPS)), dma((2, 2, GROUPS)), dma((2, GROUPS)), dma((2, GROUPS)),
            dma((GROUPS,)), dma((GROUPS,)), dma((1,)), dma((1,)),
            dma((GROUPS,)), dma((GROUPS,)), dma((GROUPS,)), dma((GROUPS,)),
        ],
        compiler_params=pltpu.CompilerParams(
            collective_id=0, has_side_effects=True, vmem_limit_bytes=58 * 2**20
        ),
    )(
        adapter_inputs.reshape(seqs, LEN, rank),
        routes.reshape(seqs, 1, LEN),
        input_eigen_basis.transpose(0, 2, 1).reshape(rows, rank),
        out_grads.reshape(seqs, LEN, width),
        output_eigen_basis.reshape(GROUPS, width, width),
        eigen_values.reshape(rows, width),
        query_grads.reshape(queries, rows, width),
    )


def solution(mesh):
    placed = (
        P("dp", None),
        P("dp", "mp"),
        P("dp"),
        P(),
        P(None, "mp"),
        P(None, None, "mp"),
        P("dp", None, None, "mp"),
    )
    return jax.shard_map(
        local, mesh=mesh, in_specs=placed, out_specs=P("dp", None), check_vma=False
    )
```

time: 427 us -> 92.3 us (0.22)
  waiting for transfers between devices: 271 us -> 0 us
  Pallas kernels: 0 us -> 87.1 us
  matrix products: 45.2 us -> 0 us
  local copies, waits for them, and re-layouts: 48.6 us -> 4.93 us
  other arithmetic: 28.7 us -> 0 us
  blocking collectives: 18.8 us -> 0 us
  between operations: 13.5 us -> 0.01 us
    all_gather x2 -> x0, waiting for transfers between devices: 271 us -> none  [the longest x1 140 us: local(): piece = lax.all_gather(query_grads, 'dp', axis=0, tiled=True)]
    pallas_call x0 -> x1, Pallas kernels: none -> 87.1 us  [local(): pl.pallas_call(functools.partial(kernel, dims), out_shape=jax.ShapeDtypeS...]
    dot_general x3 -> x0, matrix products: 44.4 us -> none  [the longest x1 27.2 us: local(): part = jnp.dot(train_flat, precond.T, precision=lax.Precision.HIGHEST)]
    unnamed x9 -> x2, local copies, waits for them, and re-layouts: 47.5 us -> 3.39 us
    div x1 -> x0, other arithmetic: 27.2 us -> none  [local(): piece.astype(jnp.float32) / shifted[None]]
    psum x1 -> x0, blocking collectives: 18.8 us -> none  [local(): totals = lax.psum(part, 'mp')]
  transfers between devices with their start and end apart: 2 -> 0, of which waited for: 2 -> 0; matrix products, arithmetic and copies ran while one was open for 3% -> 0% of each run, Pallas kernels for 0% -> 0%
where the time goes in v1:
time: 92.3 us; the launch traced here: 92 us
  Pallas kernels  87.1 us (94%)
  local copies, waits for them, and re-layouts  4.93 us (5%)
    pallas_call x1, Pallas kernels, local(): pl.pallas_call(functools.partial(kernel, dims), out_shape=jax.ShapeDtypeS...  87.1 us
    unnamed x2, local copies, waits for them, and re-layouts  3.39 us

profile of v1, /device:TPU:0, one launch (start us, length us, event | category | flops | bytes accessed | tf_op | source)
XLA Modules:
  0.0 92.0 jit_solution(9835881924012047083)
XLA Ops:
  0.0 1.5 %copy.9 = f32[2,64,64]{2,1,0:T(8,128)} copy(f32[2,64,64]{1,2,0:T(8,128)} %bitcast.14) | data formatting | bytes 65536 | tf_op jit(solution)/shard_map/transpose | solution.py:379
  1.5 2.1 %copy.8 = bf16[3072,64]{1,0:T(8,128)(2,1)} copy(bf16[3072,64]{0,1:T(8,128)(2,1)} %param.7) | data formatting | bytes 786432 | tf_op args[0]
  3.7 87.1 %shard_map.73 = f32[3,96]{1,0:T(4,128)} custom-call(bf16[3,1024,64]{2,1,0:T(8,128)(2,1)} %bitcast.10, s32[3,1,1024]{2,1,0:T(1,128)} %bitcast.15, f32[128,64]{1,0:T(8,128)} %bitcast.13, bf16[3,1024,1024]{2,1,0:T(8,128)(2,1)} %bitcast.9, bf16[8,1024,1024]{2,1,0:T(8,128)(2,1)} %bitcast.8, f32[128,1024]{1,0:T(8,128)} %bitcast.12, bf16[6,128,1024]{2,1,0:T(8,128)(2,1)} %bitcast.11), custom_call_target="tpu_custom_call" | custom-call | tf_op jit(solution)/shard_map/pallas_call | solution.py:348
  90.8 1.2 %copy.11 = f32[3,96]{1,0:T(4,128)} copy(f32[3,96]{1,0:T(4,128)} %shard_map.73) | data formatting | bytes 2304

commit v2 on v0

v2 whole, which is shorter than its diff:
```python
import functools
import math

import jax
import jax.numpy as jnp
from jax import lax
from jax.experimental import pallas as pl
from jax.experimental.pallas import tpu as pltpu
from jax.sharding import PartitionSpec as P

LEN = 1024
LANES = 128
DAMPING = 0.1
F32, BF16 = jnp.float32, jnp.bfloat16

GROUPS = 8
CORES = 2
YS = 4
ORDER = (0, 1, 7, 2, 6, 3, 5, 4)
EARLY = (0, 1)
NT = (((1,), (1,)), ((), ()))


def kernel(
    dims,
    a_ref, routes_ref, basis_ref, g_hbm, u_hbm, eig_hbm, q_hbm,
    out_ref,
    g_v, u_v, eig_v, raw, gat, qbuf, qwide, qrow, acc, part, got,
    g_sem, u_sem, l_sem,
    a_send, a_recv, z_send, z_recv, e_send, e_recv, y_send, y_recv, f_send, f_recv,
    q_send, q_recv, c_send, c_recv, r_send, r_recv,
):
    seqs, rows, rank, experts, width, queries, blk = dims
    piece = seqs * blk
    dp, mp = lax.axis_index("dp"), lax.axis_index("mp")
    s, k = dp // CORES, dp % CORES
    y, l = mp // 2, mp % 2

    def dp_peer(b):
        return {"dp": b * CORES + k, "mp": mp}

    def mp_peer(m):
        return {"dp": dp, "mp": m}

    def at(dy, dl):
        return ((y + dy) % YS) * 2 + (l + dl) % 2

    def remote(src, dst, send, recv, dev):
        return pltpu.make_async_remote_copy(
            src_ref=src, dst_ref=dst, send_sem=send, recv_sem=recv, device_id=dev
        )

    partner = {"dp": s * CORES + 1 - k, "mp": mp}

    for n in range(seqs):
        pltpu.make_async_copy(g_hbm.at[n], g_v.at[n], g_sem.at[n]).start()
    eig_copy = pltpu.make_async_copy(
        eig_hbm.at[pl.ds(pl.multiple_of(s * blk, blk), blk), :], eig_v, l_sem.at[0]
    )
    eig_copy.start()

    barrier = pltpu.get_barrier_semaphore()
    greeted = [dp_peer((s + o) % GROUPS) for o in range(1, GROUPS)]
    greeted += [
        {"dp": (s + o) % GROUPS * CORES + k, "mp": at(0, 1)} for o in range(1, GROUPS, 2)
    ]
    greeted += [mp_peer(at(1, 0)), mp_peer(at(YS - 1, 0)), mp_peer(at(0, 1)), partner]
    for device in greeted:
        pl.semaphore_signal(barrier, inc=1, device_id=device)

    for m in range(GROUPS):
        pltpu.make_async_copy(u_hbm.at[m], u_v.at[m], u_sem.at[m]).start()

    basis = jnp.concatenate([basis_ref[e] for e in range(experts)], axis=1).T
    parts, rest = [], basis
    for _ in range(3):
        parts.append(rest.astype(BF16))
        rest = rest - parts[-1].astype(F32)
    row_expert = lax.broadcasted_iota(jnp.int32, (rows, 1), 0) // rank

    def sequence(n, carry):
        pltpu.make_async_copy(g_hbm.at[n], g_v.at[n], g_sem.at[n]).wait()
        a = a_ref[:, pl.ds(pl.multiple_of(n * LEN, LEN), LEN)]
        spread = jnp.dot(parts[2], a, preferred_element_type=F32)
        spread += jnp.dot(parts[1], a, preferred_element_type=F32)
        spread += jnp.dot(parts[0], a, preferred_element_type=F32)
        rotated = jnp.where(routes_ref[n] == row_expert, spread, 0.0).astype(BF16)
        sums = jnp.dot(rotated, g_v[n], preferred_element_type=F32).astype(BF16)
        raw[:, pl.ds(pl.multiple_of(n * blk, blk), blk), :] = sums.reshape(GROUPS, blk, width)
        return carry

    lax.fori_loop(0, seqs, sequence, 0)
    gat[mp, 0] = raw[s]

    pl.semaphore_wait(barrier, len(greeted))

    first_col = [o % 2 for o in ORDER]
    direct = [i for i in range(GROUPS) if i not in EARLY]
    f_way = {(i, first_col[i]): i % 2 for i in range(GROUPS)}
    f_way.update({(i, 1 - first_col[i]): n % 2 for n, i in enumerate(direct)})

    def slot(dy, col, i):
        return gat.at[at(dy % YS, col), i]

    def a_copy(i):
        b = (s + ORDER[i]) % GROUPS
        device = {"dp": b * CORES + k, "mp": at(0, first_col[i])}
        return remote(raw.at[b], gat.at[mp, i], a_send.at[i], a_recv.at[i], device)

    def a_landed(i):
        here = slot(0, first_col[i], i)
        return remote(here, here, a_send.at[i], a_recv.at[i], partner)

    def z_copy(i):
        here = slot(0, first_col[i], i)
        return remote(here, here, z_send.at[i], z_recv.at[i], mp_peer(at(0, 1)))

    def z_landed(i):
        here = slot(0, 1 - first_col[i], i)
        return remote(here, here, z_send.at[i], z_recv.at[i], mp_peer(at(0, 1)))

    def way_peer(way):
        return mp_peer(at(1 if way == 0 else YS - 1, 0))

    def y_copy(i, col, way):
        here = slot(0, col, i)
        return remote(here, here, y_send.at[col, way, i], y_recv.at[col, way, i], way_peer(way))

    def y_landed(i, col, way):
        here = slot(-1 if way == 0 else 1, col, i)
        return remote(here, here, y_send.at[col, way, i], y_recv.at[col, way, i], way_peer(way))

    def f_copy(i, col):
        way = f_way[i, col]
        here = slot(-1 if way == 0 else 1, col, i)
        return remote(here, here, f_send.at[col, i], f_recv.at[col, i], way_peer(way))

    def f_landed(i, col):
        here = slot(2, col, i)
        return remote(here, here, f_send.at[col, i], f_recv.at[col, i], partner)

    def e_copy(i, dy):
        here = slot(dy, first_col[i], i)
        n = EARLY.index(i)
        return remote(here, here, e_send.at[n, dy % YS], e_recv.at[n, dy % YS], mp_peer(at(0, 1)))

    def e_landed(i, dy):
        here = slot(dy, 1 - first_col[i], i)
        n = EARLY.index(i)
        return remote(here, here, e_send.at[n, dy % YS], e_recv.at[n, dy % YS], partner)

    def q_source(b):
        return q_hbm.at[:, pl.ds(pl.multiple_of(b * blk, blk), blk), :]

    def q_copy(i):
        b = (s + ORDER[i]) % GROUPS
        return remote(q_source(b), qbuf.at[s, k], q_send.at[i], q_recv.at[i], dp_peer(b))

    def q_landed(i):
        here = qbuf.at[(s + GROUPS - ORDER[i]) % GROUPS, k]
        return remote(here, here, q_send.at[i], q_recv.at[i], partner)

    def both_ways(i, col):
        y_copy(i, col, 0).start()
        y_copy(i, col, 1).start()

    def forward(i, col):
        y_landed(i, col, f_way[i, col]).wait_recv()
        f_copy(i, col).start()

    def other_way(i, col):
        y_landed(i, col, 1 - f_way[i, col]).wait_recv()

    def multiply(m, low=0, high=GROUPS, first=False, wait=True):
        if wait:
            pltpu.make_async_copy(u_hbm.at[m], u_v.at[m], u_sem.at[m]).wait()
        step = 256

        def column(c, carry):
            cols = pl.ds(pl.multiple_of(c * step, step), step)
            product = jnp.dot(
                gat[m, low:high].reshape((high - low) * piece, width), u_v[m, :, cols],
                preferred_element_type=F32,
            )
            own = slice(low * piece, high * piece)
            for half in range(step // LANES):
                lanes = c * (step // LANES) + half
                term = product[:, half * LANES : (half + 1) * LANES]
                acc[lanes, own] = term if first else acc[lanes, own] + term
            return carry

        lax.fori_loop(0, width // step, column, 0)

    for i in range(1, GROUPS):
        a_copy(i).start()
    for i in range(GROUPS):
        if i:
            a_landed(i).wait_recv()
        both_ways(i, first_col[i])
        z_copy(i).start()

    q_own = pltpu.make_async_copy(q_source(s), qbuf.at[s, k], l_sem.at[1])
    q_own.start()
    for i in range(1, GROUPS):
        q_copy(i).start()

    for i in range(GROUPS):
        forward(i, first_col[i])
        if i in EARLY:
            other_way(i, first_col[i])
            e_copy(i, 1).start()
            e_copy(i, -1).start()
        z_landed(i).wait_recv()
        if i in direct:
            both_ways(i, 1 - first_col[i])
    multiply(at(0, 0), first=True)
    for i in EARLY:
        f_landed(i, first_col[i]).wait_recv()
        e_copy(i, 2).start()
    multiply(at(0, 1))
    for i in direct[: len(direct) // 2]:
        forward(i, 1 - first_col[i])

    for i in range(1, GROUPS):
        q_landed(i).wait_recv()
    q_own.wait()
    c_copy = remote(qbuf.at[:, k], qbuf.at[:, k], c_send.at[0], c_recv.at[0], partner)
    c_copy.start()
    for i in direct[len(direct) // 2 :]:
        forward(i, 1 - first_col[i])
    remote(qbuf.at[:, 1 - k], qbuf.at[:, 1 - k], c_send.at[0], c_recv.at[0], partner).wait_recv()
    total = GROUPS * CORES * queries

    def widen(g, carry):
        chunk = queries * CORES * blk
        own = pl.ds(pl.multiple_of(g * chunk, chunk), chunk)
        for lanes in range(width // LANES):
            cols = qbuf[g, :, :, :, lanes * LANES : (lanes + 1) * LANES]
            qwide[lanes, own, :] = cols.reshape(chunk, LANES).astype(F32)
        return carry

    lax.fori_loop(0, GROUPS, widen, 0)

    def regroup(r, carry):
        for lanes in range(width // LANES):
            cols = qwide[lanes, pl.ds(r, total, stride=blk), :]
            qrow[r, :, lanes * LANES : (lanes + 1) * LANES] = cols.astype(BF16)
        return carry

    lax.fori_loop(0, blk, regroup, 0)
    eig_copy.wait()
    eig_v[...] = 1.0 / (eig_v[...] + DAMPING)

    for i in range(GROUPS):
        if i not in EARLY:
            other_way(i, first_col[i])
    for i in direct:
        other_way(i, 1 - first_col[i])
    for i in EARLY:
        e_landed(i, 1).wait_recv()
        e_landed(i, -1).wait_recv()
    for dy in (1, -1):
        for col in (0, 1):
            multiply(at(dy % YS, col))

    def far(i):
        if i not in EARLY:
            f_landed(i, first_col[i]).wait_recv()
        if i in direct:
            f_landed(i, 1 - first_col[i]).wait_recv()
        else:
            e_landed(i, 2).wait_recv()

    def score(low, high):
        count = (high - low) * seqs
        scores = jnp.zeros((count, total), F32)
        for r in range(blk):
            own = pl.ds(low * piece + r, count, stride=blk)
            train = jnp.concatenate([acc[lanes, own, :] for lanes in range(width // LANES)], axis=1)
            train = train.astype(BF16).astype(F32) * eig_v[r : r + 1, :]
            upper = train.astype(BF16)
            lower = (train - upper.astype(F32)).astype(BF16)
            scores += lax.dot_general(upper, qrow[r], NT, preferred_element_type=F32)
            scores += lax.dot_general(lower, qrow[r], NT, preferred_element_type=F32)
        for i in range(low, high):
            part[i, :seqs, :total] = scores[(i - low) * seqs : (i - low + 1) * seqs]

    part[...] = jnp.zeros(part.shape, F32)
    half = GROUPS // 2
    for low in (0, half):
        for i in range(low, low + half):
            far(i)
        for col in (0, 1):
            multiply(at(2, col), low, low + half, wait=low == 0)
        score(low, low + half)

    me = s * GROUPS + mp

    def r_copy(i, m):
        device = {"dp": (s + GROUPS - ORDER[i]) % GROUPS * CORES + k, "mp": m}
        return remote(part.at[i], got.at[me], r_send.at[0], r_recv.at[0], device)

    for i in range(1, GROUPS):
        r_copy(i, mp).start()

    def round_mp(o, carry):
        for i in range(GROUPS):
            r_copy(i, (mp + o) % GROUPS).start()
        return carry

    lax.fori_loop(1, GROUPS, round_mp, 0)
    got[me] = part[0]
    others = got.at[pl.ds(0, GROUPS * GROUPS - 1)]
    r_all = remote(others, others, r_send.at[0], r_recv.at[0], partner)
    r_all.wait_recv()
    scale = 1.0 / math.sqrt(LEN * rows * width * GROUPS)
    out_ref[...] = jnp.sum(got[...], axis=0)[:seqs, :total] * scale

    r_all.wait_send()
    c_copy.wait_send()
    for i in range(GROUPS):
        if i:
            a_copy(i).wait_send()
            q_copy(i).wait_send()
        z_copy(i).wait_send()
        if i in EARLY:
            for dy in (1, -1, 2):
                e_copy(i, dy).wait_send()
        for col in (0, 1):
            if (i, col) in f_way:
                y_copy(i, col, 0).wait_send()
                y_copy(i, col, 1).wait_send()
                f_copy(i, col).wait_send()


def local(adapter_inputs, out_grads, routes, input_eigen_basis, output_eigen_basis, eigen_values, query_grads):
    tokens, rank = adapter_inputs.shape
    experts = input_eigen_basis.shape[0]
    rows = experts * rank
    width = out_grads.shape[1]
    queries = query_grads.shape[0]
    seqs = tokens // LEN
    blk = rows // GROUPS
    dims = (seqs, rows, rank, experts, width, queries, blk)
    piece = seqs * blk
    total = GROUPS * CORES * queries
    vmem, hbm = pl.BlockSpec(memory_space=pltpu.VMEM), pl.BlockSpec(memory_space=pl.ANY)
    dma = pltpu.SemaphoreType.DMA
    return pl.pallas_call(
        functools.partial(kernel, dims),
        out_shape=jax.ShapeDtypeStruct((seqs, total), F32),
        in_specs=[vmem, vmem, vmem, hbm, hbm, hbm, hbm],
        out_specs=vmem,
        scratch_shapes=[
            pltpu.VMEM((seqs, LEN, width), BF16),
            pltpu.VMEM((GROUPS, width, width), BF16),
            pltpu.VMEM((blk, width), F32),
            pltpu.VMEM((GROUPS, piece, width), BF16),
            pltpu.VMEM((GROUPS, GROUPS, piece, width), BF16),
            pltpu.VMEM((GROUPS, CORES, queries, blk, width), BF16),
            pltpu.VMEM((width // LANES, total * blk, LANES), F32),
            pltpu.VMEM((blk, total, width), BF16),
            pltpu.VMEM((width // LANES, GROUPS * piece, LANES), F32),
            pltpu.VMEM((GROUPS, 4, LANES), F32),
            pltpu.VMEM((GROUPS * GROUPS, 4, LANES), F32),
            dma((seqs,)), dma((GROUPS,)), dma((2,)),
            dma((GROUPS,)), dma((GROUPS,)), dma((GROUPS,)), dma((GROUPS,)),
            dma((len(EARLY), YS)), dma((len(EARLY), YS)),
            dma((2, 2, GROUPS)), dma((2, 2, GROUPS)), dma((2, GROUPS)), dma((2, GROUPS)),
            dma((GROUPS,)), dma((GROUPS,)), dma((1,)), dma((1,)), dma((1,)), dma((1,)),
        ],
        compiler_params=pltpu.CompilerParams(
            collective_id=0, has_side_effects=True, vmem_limit_bytes=58 * 2**20
        ),
    )(
        adapter_inputs.T,
        routes.reshape(seqs, 1, LEN),
        input_eigen_basis,
        out_grads.reshape(seqs, LEN, width),
        output_eigen_basis.reshape(GROUPS, width, width),
        eigen_values.reshape(rows, width),
        query_grads.reshape(queries, rows, width),
    )


def solution(mesh):
    placed = (
        P("dp", None),
        P("dp", "mp"),
        P("dp"),
        P(),
        P(None, "mp"),
        P(None, None, "mp"),
        P("dp", None, None, "mp"),
    )
    return jax.shard_map(
        local, mesh=mesh, in_specs=placed, out_specs=P("dp", None), check_vma=False
    )
```

time: 427 us -> 87.8 us (0.21)
  waiting for transfers between devices: 271 us -> 0 us
  Pallas kernels: 0 us -> 86.4 us
  local copies, waits for them, and re-layouts: 48.6 us -> 1.26 us
  matrix products: 45.2 us -> 0 us
  other arithmetic: 28.7 us -> 0 us
  blocking collectives: 18.8 us -> 0 us
  between operations: 13.5 us -> 0.01 us
    all_gather x2 -> x0, waiting for transfers between devices: 271 us -> none  [the longest x1 140 us: local(): piece = lax.all_gather(query_grads, 'dp', axis=0, tiled=True)]
    pallas_call x0 -> x1, Pallas kernels: none -> 86.4 us  [local(): pl.pallas_call(functools.partial(kernel, dims), out_shape=jax.ShapeDtypeS...]
    unnamed x9 -> x1, local copies, waits for them, and re-layouts: 47.5 us -> 1.26 us
    dot_general x3 -> x0, matrix products: 44.4 us -> none  [the longest x1 27.2 us: local(): part = jnp.dot(train_flat, precond.T, precision=lax.Precision.HIGHEST)]
    div x1 -> x0, other arithmetic: 27.2 us -> none  [local(): piece.astype(jnp.float32) / shifted[None]]
    psum x1 -> x0, blocking collectives: 18.8 us -> none  [local(): totals = lax.psum(part, 'mp')]
  transfers between devices with their start and end apart: 2 -> 0, of which waited for: 2 -> 0; matrix products, arithmetic and copies ran while one was open for 3% -> 0% of each run, Pallas kernels for 0% -> 0%
where the time goes in v2:
time: 87.8 us; the launch traced here: 87.6 us
  Pallas kernels  86.4 us (98%)
  local copies, waits for them, and re-layouts  1.26 us (1%)
    pallas_call x1, Pallas kernels, local(): pl.pallas_call(functools.partial(kernel, dims), out_shape=jax.ShapeDtypeS...  86.4 us

profile of v2, /device:TPU:0, one launch (start us, length us, event | category | flops | bytes accessed | tf_op | source)
XLA Modules:
  0.0 87.6 jit_solution(5366157360597128276)
XLA Ops:
  0.0 86.4 %shard_map.73 = f32[3,96]{1,0:T(4,128)} custom-call(bf16[64,3072]{1,0:T(8,128)(2,1)} %bitcast.10, s32[3,1,1024]{2,1,0:T(1,128)} %bitcast.11, f32[2,64,64]{2,1,0:T(8,128)} %basis_ref.1, bf16[3,1024,1024]{2,1,0:T(8,128)(2,1)} %bitcast.7, bf16[8,1024,1024]{2,1,0:T(8,128)(2,1)} %bitcast.6, f32[128,1024]{1,0:T(8,128)} %bitcast.9, bf16[6,128,1024]{2,1,0:T(8,128)(2,1)} %bitcast.8), custom_call_target="tpu_custom_call" | custom-call | tf_op jit(solution)/shard_map/pallas_call | solution.py:349
  86.4 1.3 %copy.9 = f32[3,96]{1,0:T(4,128)} copy(f32[3,96]{1,0:T(4,128)} %shard_map.73) | data formatting | bytes 2304

commit v3 on v2

--- a/solution.py
+++ b/solution.py
@@ -17,7 +17,16 @@
 CORES = 2
 YS = 4
 ORDER = (0, 1, 7, 2, 6, 3, 5, 4)
-EARLY = (0, 1)
+EARLY = (3, 6)
+SPLIT = 4
+STEPS = (
+    ("F", 0, 0), ("Z", 0), ("A", 1), ("A", 3), ("A", 4), ("A", 2), ("Z", 1), ("A", 5), ("F", 0, 1), ("A", 7),
+    ("F", 1, 0), ("A", 6), ("Q", 1), ("Q", 2), ("Q", 7), ("Q", 5), ("Q", 6), ("Q", 4), ("Q", 3), ("F", 3, 0), ("E", 3, 1),
+    ("Z", 4), ("E", 3, 0), ("Z", 2), ("M", 0, 0), ("F", 4, 0), ("Z", 5), ("F", 2, 0), ("F", 1, 1), ("F", 5, 0),
+    ("F", 7, 0), ("Z", 7), ("E", 6, 1), ("F", 6, 0), ("E", 6, 0), ("G", 3), ("F", 4, 1), ("F", 2, 1), ("C",),
+    ("M", 1, 0), ("F", 5, 1), ("M", 0, 2), ("M", 0, 1), ("R",), ("M", 1, 1), ("G", 6), ("F", 7, 1), ("M", 1, 2),
+    ("M", 0, 3), ("M", 1, 3),
+)
 NT = (((1,), (1,)), ((), ()))
 
 
@@ -68,9 +77,6 @@
     for device in greeted:
         pl.semaphore_signal(barrier, inc=1, device_id=device)
 
-    for m in range(GROUPS):
-        pltpu.make_async_copy(u_hbm.at[m], u_v.at[m], u_sem.at[m]).start()
-
     basis = jnp.concatenate([basis_ref[e] for e in range(experts)], axis=1).T
     parts, rest = [], basis
     for _ in range(3):
@@ -78,21 +84,15 @@
         rest = rest - parts[-1].astype(F32)
     row_expert = lax.broadcasted_iota(jnp.int32, (rows, 1), 0) // rank
 
-    def sequence(n, carry):
+    def sequence(n):
         pltpu.make_async_copy(g_hbm.at[n], g_v.at[n], g_sem.at[n]).wait()
-        a = a_ref[:, pl.ds(pl.multiple_of(n * LEN, LEN), LEN)]
+        a = a_ref[:, n * LEN : (n + 1) * LEN]
         spread = jnp.dot(parts[2], a, preferred_element_type=F32)
         spread += jnp.dot(parts[1], a, preferred_element_type=F32)
         spread += jnp.dot(parts[0], a, preferred_element_type=F32)
         rotated = jnp.where(routes_ref[n] == row_expert, spread, 0.0).astype(BF16)
         sums = jnp.dot(rotated, g_v[n], preferred_element_type=F32).astype(BF16)
-        raw[:, pl.ds(pl.multiple_of(n * blk, blk), blk), :] = sums.reshape(GROUPS, blk, width)
-        return carry
-
-    lax.fori_loop(0, seqs, sequence, 0)
-    gat[mp, 0] = raw[s]
-
-    pl.semaphore_wait(barrier, len(greeted))
+        raw[:, n * blk : (n + 1) * blk, :] = sums.reshape(GROUPS, blk, width)
 
     first_col = [o % 2 for o in ORDER]
     direct = [i for i in range(GROUPS) if i not in EARLY]
@@ -102,17 +102,18 @@
     def slot(dy, col, i):
         return gat.at[at(dy % YS, col), i]
 
-    def a_copy(i):
+    def a_copy(i, low=0, high=seqs):
         b = (s + ORDER[i]) % GROUPS
         device = {"dp": b * CORES + k, "mp": at(0, first_col[i])}
-        return remote(raw.at[b], gat.at[mp, i], a_send.at[i], a_recv.at[i], device)
+        own = pl.ds(low * blk, (high - low) * blk)
+        return remote(raw.at[b, own], gat.at[mp, i, own], a_send.at[i], a_recv.at[i], device)
 
     def a_landed(i):
         here = slot(0, first_col[i], i)
         return remote(here, here, a_send.at[i], a_recv.at[i], partner)
 
-    def z_copy(i):
-        here = slot(0, first_col[i], i)
+    def z_copy(i, low=0, high=seqs):
+        here = slot(0, first_col[i], i).at[pl.ds(low * blk, (high - low) * blk)]
         return remote(here, here, z_send.at[i], z_recv.at[i], mp_peer(at(0, 1)))
 
     def z_landed(i):
@@ -122,8 +123,8 @@
     def way_peer(way):
         return mp_peer(at(1 if way == 0 else YS - 1, 0))
 
-    def y_copy(i, col, way):
-        here = slot(0, col, i)
+    def y_copy(i, col, way, low=0, high=seqs):
+        here = slot(0, col, i).at[pl.ds(low * blk, (high - low) * blk)]
         return remote(here, here, y_send.at[col, way, i], y_recv.at[col, way, i], way_peer(way))
 
     def y_landed(i, col, way):
@@ -171,64 +172,43 @@
     def other_way(i, col):
         y_landed(i, col, 1 - f_way[i, col]).wait_recv()
 
-    def multiply(m, low=0, high=GROUPS, first=False, wait=True):
-        if wait:
-            pltpu.make_async_copy(u_hbm.at[m], u_v.at[m], u_sem.at[m]).wait()
-        step = 256
-
-        def column(c, carry):
-            cols = pl.ds(pl.multiple_of(c * step, step), step)
+    def multiply(dy, low, high, first, wait):
+        def column(col, carry):
+            m = at(dy, col)
+            if wait:
+                pltpu.make_async_copy(u_hbm.at[m], u_v.at[m], u_sem.at[m]).wait()
             product = jnp.dot(
-                gat[m, low:high].reshape((high - low) * piece, width), u_v[m, :, cols],
-                preferred_element_type=F32,
+                gat[m, low:high].reshape((high - low) * piece, width), u_v[m], preferred_element_type=F32
             )
             own = slice(low * piece, high * piece)
-            for half in range(step // LANES):
-                lanes = c * (step // LANES) + half
-                term = product[:, half * LANES : (half + 1) * LANES]
-                acc[lanes, own] = term if first else acc[lanes, own] + term
+            for lanes in range(width // LANES):
+                acc[lanes, own] += product[:, lanes * LANES : (lanes + 1) * LANES]
             return carry
 
-        lax.fori_loop(0, width // step, column, 0)
-
-    for i in range(1, GROUPS):
-        a_copy(i).start()
-    for i in range(GROUPS):
-        if i:
-            a_landed(i).wait_recv()
-        both_ways(i, first_col[i])
-        z_copy(i).start()
-
+        if first:
+            acc[:, low * piece : high * piece] = jnp.zeros((width // LANES, (high - low) * piece, LANES), F32)
+        lax.fori_loop(0, 2, column, 0)
+
+    for n in range(seqs):
+        sequence(n)
+        if n == 0:
+            pl.semaphore_wait(barrier, len(greeted))
+        for i in range(1, GROUPS):
+            a_copy(i, n, n + 1).start()
+        gat[mp, 0, n * blk : (n + 1) * blk] = raw[s, n * blk : (n + 1) * blk]
+        y_copy(0, first_col[0], 0, n, n + 1).start()
+        y_copy(0, first_col[0], 1, n, n + 1).start()
+        z_copy(0, n, n + 1).start()
     q_own = pltpu.make_async_copy(q_source(s), qbuf.at[s, k], l_sem.at[1])
     q_own.start()
-    for i in range(1, GROUPS):
-        q_copy(i).start()
-
-    for i in range(GROUPS):
-        forward(i, first_col[i])
-        if i in EARLY:
-            other_way(i, first_col[i])
-            e_copy(i, 1).start()
-            e_copy(i, -1).start()
-        z_landed(i).wait_recv()
-        if i in direct:
-            both_ways(i, 1 - first_col[i])
-    multiply(at(0, 0), first=True)
-    for i in EARLY:
-        f_landed(i, first_col[i]).wait_recv()
-        e_copy(i, 2).start()
-    multiply(at(0, 1))
-    for i in direct[: len(direct) // 2]:
-        forward(i, 1 - first_col[i])
-
-    for i in range(1, GROUPS):
-        q_landed(i).wait_recv()
-    q_own.wait()
+    for m in range(GROUPS):
+        pltpu.make_async_copy(u_hbm.at[m], u_v.at[m], u_sem.at[m]).start()
+    acc[:, GROUPS * piece :] = jnp.zeros((width // LANES, blk * 4, LANES), F32)
+    part[...] = jnp.zeros(part.shape, F32)
+    eig_copy.wait()
+    eig_v[...] = 1.0 / (eig_v[...] + DAMPING)
     c_copy = remote(qbuf.at[:, k], qbuf.at[:, k], c_send.at[0], c_recv.at[0], partner)
-    c_copy.start()
-    for i in direct[len(direct) // 2 :]:
-        forward(i, 1 - first_col[i])
-    remote(qbuf.at[:, 1 - k], qbuf.at[:, 1 - k], c_send.at[0], c_recv.at[0], partner).wait_recv()
+    c_here = remote(qbuf.at[:, 1 - k], qbuf.at[:, 1 - k], c_send.at[0], c_recv.at[0], partner)
     total = GROUPS * CORES * queries
 
     def widen(g, carry):
@@ -239,60 +219,29 @@
             qwide[lanes, own, :] = cols.reshape(chunk, LANES).astype(F32)
         return carry
 
-    lax.fori_loop(0, GROUPS, widen, 0)
-
     def regroup(r, carry):
         for lanes in range(width // LANES):
             cols = qwide[lanes, pl.ds(r, total, stride=blk), :]
             qrow[r, :, lanes * LANES : (lanes + 1) * LANES] = cols.astype(BF16)
         return carry
 
-    lax.fori_loop(0, blk, regroup, 0)
-    eig_copy.wait()
-    eig_v[...] = 1.0 / (eig_v[...] + DAMPING)
-
-    for i in range(GROUPS):
-        if i not in EARLY:
-            other_way(i, first_col[i])
-    for i in direct:
-        other_way(i, 1 - first_col[i])
-    for i in EARLY:
-        e_landed(i, 1).wait_recv()
-        e_landed(i, -1).wait_recv()
-    for dy in (1, -1):
-        for col in (0, 1):
-            multiply(at(dy % YS, col))
-
-    def far(i):
-        if i not in EARLY:
-            f_landed(i, first_col[i]).wait_recv()
-        if i in direct:
-            f_landed(i, 1 - first_col[i]).wait_recv()
-        else:
-            e_landed(i, 2).wait_recv()
-
     def score(low, high):
-        count = (high - low) * seqs
-        scores = jnp.zeros((count, total), F32)
-        for r in range(blk):
-            own = pl.ds(low * piece + r, count, stride=blk)
-            train = jnp.concatenate([acc[lanes, own, :] for lanes in range(width // LANES)], axis=1)
-            train = train.astype(BF16).astype(F32) * eig_v[r : r + 1, :]
-            upper = train.astype(BF16)
-            lower = (train - upper.astype(F32)).astype(BF16)
-            scores += lax.dot_general(upper, qrow[r], NT, preferred_element_type=F32)
-            scores += lax.dot_general(lower, qrow[r], NT, preferred_element_type=F32)
+        padded, step = 16, 4
+
+        def some_rows(g, scores):
+            for r in [g * step + n for n in range(step)]:
+                own = pl.ds(low * piece + r, padded, stride=blk)
+                train = jnp.concatenate([acc[lanes, own, :] for lanes in range(width // LANES)], axis=1)
+                train = train.astype(BF16).astype(F32) * eig_v[pl.ds(r, 1), :]
+                upper = train.astype(BF16).astype(F32)
+                both = jnp.concatenate([upper, train - upper], axis=0).astype(BF16)
+                scores += lax.dot_general(both, qrow[r], NT, preferred_element_type=F32)
+            return scores
+
+        scores = lax.fori_loop(0, blk // step, some_rows, jnp.zeros((2 * padded, total), F32))
+        scores = scores[:padded] + scores[padded:]
         for i in range(low, high):
             part[i, :seqs, :total] = scores[(i - low) * seqs : (i - low + 1) * seqs]
-
-    part[...] = jnp.zeros(part.shape, F32)
-    half = GROUPS // 2
-    for low in (0, half):
-        for i in range(low, low + half):
-            far(i)
-        for col in (0, 1):
-            multiply(at(2, col), low, low + half, wait=low == 0)
-        score(low, low + half)
 
     me = s * GROUPS + mp
 
@@ -300,15 +249,82 @@
         device = {"dp": (s + GROUPS - ORDER[i]) % GROUPS * CORES + k, "mp": m}
         return remote(part.at[i], got.at[me], r_send.at[0], r_recv.at[0], device)
 
-    for i in range(1, GROUPS):
-        r_copy(i, mp).start()
-
-    def round_mp(o, carry):
-        for i in range(GROUPS):
-            r_copy(i, (mp + o) % GROUPS).start()
-        return carry
-
-    lax.fori_loop(1, GROUPS, round_mp, 0)
+    def send_scores(low, high):
+        for o in (4, 5, 3, 2, 6, 1, 7, 0):
+            for i in range(high - 1, low - 1, -1):
+                if i or o:
+                    r_copy(i, (mp + o) % GROUPS).start()
+
+    waited, loaded = set(), set()
+
+    def wait(copy, *name):
+        if name not in waited:
+            waited.add(name)
+            copy(*name[1:]).wait_recv()
+
+    def y_wait(i, second, way):
+        wait(lambda *_: y_landed(i, first_col[i] ^ second, way), "y", i, second, way)
+
+    def multiply_half(part_of, source):
+        low, high = (0, SPLIT) if part_of == 0 else (SPLIT, GROUPS)
+        dy = (0, -1, 1, 2)[source]
+        for i in range(low, high):
+            if source == 0:
+                if i:
+                    wait(a_landed, "a", i)
+                wait(z_landed, "z", i)
+            elif source == 3:
+                wait(lambda *_: f_landed(i, first_col[i]), "f", i, 0)
+                if i in EARLY:
+                    e_landed(i, 2).wait_recv()
+                else:
+                    wait(lambda *_: f_landed(i, 1 - first_col[i]), "f", i, 1)
+            else:
+                y_wait(i, 0, source - 1)
+                if i in EARLY:
+                    e_landed(i, dy).wait_recv()
+                else:
+                    y_wait(i, 1, source - 1)
+        multiply(dy % YS, low, high, source == 0, dy not in loaded)
+        loaded.add(dy)
+        if source == 3:
+            score(low, high)
+            send_scores(low, high)
+
+    for step, *arg in STEPS:
+        if step == "A":
+            wait(a_landed, "a", arg[0])
+            both_ways(arg[0], first_col[arg[0]])
+            z_copy(arg[0]).start()
+        elif step == "Z":
+            wait(z_landed, "z", arg[0])
+            both_ways(arg[0], 1 - first_col[arg[0]])
+        elif step == "F":
+            i, second = arg
+            y_wait(i, second, f_way[i, first_col[i] ^ second])
+            f_copy(i, first_col[i] ^ second).start()
+        elif step == "E":
+            i, way = arg
+            y_wait(i, 0, way)
+            e_copy(i, -1 if way == 0 else 1).start()
+        elif step == "G":
+            i = arg[0]
+            wait(lambda *_: f_landed(i, first_col[i]), "f", i, 0)
+            e_copy(i, 2).start()
+        elif step == "Q":
+            q_copy(arg[0]).start()
+        elif step == "C":
+            for i in range(1, GROUPS):
+                q_landed(i).wait_recv()
+            q_own.wait()
+            c_copy.start()
+        elif step == "R":
+            c_here.wait_recv()
+            lax.fori_loop(0, GROUPS, widen, 0)
+            lax.fori_loop(0, blk, regroup, 0)
+        else:
+            multiply_half(*arg)
+
     got[me] = part[0]
     others = got.at[pl.ds(0, GROUPS * GROUPS - 1)]
     r_all = remote(others, others, r_send.at[0], r_recv.at[0], partner)
@@ -360,7 +376,7 @@
             pltpu.VMEM((GROUPS, CORES, queries, blk, width), BF16),
             pltpu.VMEM((width // LANES, total * blk, LANES), F32),
             pltpu.VMEM((blk, total, width), BF16),
-            pltpu.VMEM((width // LANES, GROUPS * piece, LANES), F32),
+            pltpu.VMEM((width // LANES, GROUPS * piece + blk * 4, LANES), F32),
             pltpu.VMEM((GROUPS, 4, LANES), F32),
             pltpu.VMEM((GROUPS * GROUPS, 4, LANES), F32),
             dma((seqs,)), dma((GROUPS,)), dma((2,)),

time: 87.8 us -> 80.5 us (0.917)
  Pallas kernels: 86.4 us -> 79 us
    pallas_call x1, Pallas kernels: 86.4 us -> 79 us  [local(): pl.pallas_call(functools.partial(kernel, dims), out_shape=jax.ShapeDtypeS...]
where the time goes in v3:
time: 80.5 us; the launch traced here: 80.3 us
  Pallas kernels  79 us (98%)
  local copies, waits for them, and re-layouts  1.26 us (2%)
    pallas_call x1, Pallas kernels, local(): pl.pallas_call(functools.partial(kernel, dims), out_shape=jax.ShapeDtypeS...  79 us

profile of v3, /device:TPU:0, one launch (start us, length us, event | category | flops | bytes accessed | tf_op | source)
XLA Modules:
  0.0 80.3 jit_solution(16217311050557843238)
XLA Ops:
  0.0 79.0 %shard_map.73 = f32[3,96]{1,0:T(4,128)} custom-call(bf16[64,3072]{1,0:T(8,128)(2,1)} %bitcast.10, s32[3,1,1024]{2,1,0:T(1,128)} %bitcast.11, f32[2,64,64]{2,1,0:T(8,128)} %basis_ref.1, bf16[3,1024,1024]{2,1,0:T(8,128)(2,1)} %bitcast.7, bf16[8,1024,1024]{2,1,0:T(8,128)(2,1)} %bitcast.6, f32[128,1024]{1,0:T(8,128)} %bitcast.9, bf16[6,128,1024]{2,1,0:T(8,128)(2,1)} %bitcast.8), custom_call_target="tpu_custom_call" | custom-call | tf_op jit(solution)/shard_map/pallas_call | solution.py:365
  79.1 1.3 %copy.9 = f32[3,96]{1,0:T(4,128)} copy(f32[3,96]{1,0:T(4,128)} %shard_map.73) | data formatting | bytes 2304

commit v4 on v3

--- a/solution.py
+++ b/solution.py
@@ -16,16 +16,20 @@
 GROUPS = 8
 CORES = 2
 YS = 4
-ORDER = (0, 1, 7, 2, 6, 3, 5, 4)
-EARLY = (3, 6)
-SPLIT = 4
+ORDER = (0, 2, 6, 4, 1, 7, 3, 5)
+EARLY = (1, 7)
+HALF = 4
+SECOND_WAY = {0: 0, 2: 1, 3: 1, 4: 1, 5: 0, 6: 0}
 STEPS = (
-    ("F", 0, 0), ("Z", 0), ("A", 1), ("A", 3), ("A", 4), ("A", 2), ("Z", 1), ("A", 5), ("F", 0, 1), ("A", 7),
-    ("F", 1, 0), ("A", 6), ("Q", 1), ("Q", 2), ("Q", 7), ("Q", 5), ("Q", 6), ("Q", 4), ("Q", 3), ("F", 3, 0), ("E", 3, 1),
-    ("Z", 4), ("E", 3, 0), ("Z", 2), ("M", 0, 0), ("F", 4, 0), ("Z", 5), ("F", 2, 0), ("F", 1, 1), ("F", 5, 0),
-    ("F", 7, 0), ("Z", 7), ("E", 6, 1), ("F", 6, 0), ("E", 6, 0), ("G", 3), ("F", 4, 1), ("F", 2, 1), ("C",),
-    ("M", 1, 0), ("F", 5, 1), ("M", 0, 2), ("M", 0, 1), ("R",), ("M", 1, 1), ("G", 6), ("F", 7, 1), ("M", 1, 2),
-    ("M", 0, 3), ("M", 1, 3),
+    ("F", 0, 0), ("Z", 0), ("A", 1), ("A", 2), ("A", 6), ("A", 7), ("Z", 1), ("A", 3), ("F", 0, 1), ("A", 4),
+    ("F", 1, 0), ("A", 5), ("Q", 1), ("Q", 7), ("Q", 4), ("Q", 3), ("Q", 5), ("Q", 6), ("Q", 2), ("F", 2, 0),
+    ("E", 2, 1), ("Z", 6), ("E", 2, 0), ("Z", 7), ("F", 6, 0), ("Z", 3), ("F", 7, 0), ("F", 1, 1), ("F", 3, 0),
+    ("F", 4, 0), ("Z", 4), ("M", 1, 0, 0), ("M", 0, 0, 0), ("E", 5, 1), ("F", 5, 0), ("E", 5, 0), ("M", 0, 1, 0),
+    ("M", 0, 2, 0), ("G", 2), ("F", 6, 1), ("M", 1, 1, 0), ("M", 1, 2, 0), ("F", 7, 1), ("C", 0), ("C", 1), ("C", 7),
+    ("C", 4), ("C", 3), ("C", 5), ("C", 6), ("C", 2), ("M", 1, 0, 1), ("M", 0, 0, 1), ("R", 0), ("R", 1), ("R", 7),
+    ("R", 4), ("F", 3, 1), ("M", 1, 3, 0), ("M", 0, 3, 0), ("R", 3), ("R", 5), ("R", 6), ("R", 2), ("M", 0, 1, 1),
+    ("M", 0, 2, 1), ("G", 5), ("F", 4, 1), ("M", 1, 1, 1), ("M", 1, 2, 1), ("M", 1, 3, 1), ("S", 1), ("M", 0, 3, 1),
+    ("S", 0),
 )
 NT = (((1,), (1,)), ((), ()))
 
@@ -96,8 +100,8 @@
 
     first_col = [o % 2 for o in ORDER]
     direct = [i for i in range(GROUPS) if i not in EARLY]
-    f_way = {(i, first_col[i]): i % 2 for i in range(GROUPS)}
-    f_way.update({(i, 1 - first_col[i]): n % 2 for n, i in enumerate(direct)})
+    f_way = {(i, first_col[i]): (i + i // HALF) % 2 for i in range(GROUPS)}
+    f_way.update({(i, 1 - first_col[i]): SECOND_WAY[i] for i in direct})
 
     def slot(dy, col, i):
         return gat.at[at(dy % YS, col), i]
@@ -172,22 +176,14 @@
     def other_way(i, col):
         y_landed(i, col, 1 - f_way[i, col]).wait_recv()
 
-    def multiply(dy, low, high, first, wait):
-        def column(col, carry):
-            m = at(dy, col)
-            if wait:
-                pltpu.make_async_copy(u_hbm.at[m], u_v.at[m], u_sem.at[m]).wait()
-            product = jnp.dot(
-                gat[m, low:high].reshape((high - low) * piece, width), u_v[m], preferred_element_type=F32
-            )
-            own = slice(low * piece, high * piece)
-            for lanes in range(width // LANES):
-                acc[lanes, own] += product[:, lanes * LANES : (lanes + 1) * LANES]
-            return carry
-
-        if first:
-            acc[:, low * piece : high * piece] = jnp.zeros((width // LANES, (high - low) * piece, LANES), F32)
-        lax.fori_loop(0, 2, column, 0)
+    def multiply(m, low, high, first):
+        product = jnp.dot(
+            gat[m, low:high].reshape((high - low) * piece, width), u_v[m], preferred_element_type=F32
+        )
+        own = slice(low * piece, high * piece)
+        for lanes in range(width // LANES):
+            term = product[:, lanes * LANES : (lanes + 1) * LANES]
+            acc[lanes, own] = term if first else acc[lanes, own] + term
 
     for n in range(seqs):
         sequence(n)
@@ -205,28 +201,39 @@
         pltpu.make_async_copy(u_hbm.at[m], u_v.at[m], u_sem.at[m]).start()
     acc[:, GROUPS * piece :] = jnp.zeros((width // LANES, blk * 4, LANES), F32)
     part[...] = jnp.zeros(part.shape, F32)
+    qwide[...] = jnp.zeros(qwide.shape, F32)
     eig_copy.wait()
     eig_v[...] = 1.0 / (eig_v[...] + DAMPING)
-    c_copy = remote(qbuf.at[:, k], qbuf.at[:, k], c_send.at[0], c_recv.at[0], partner)
-    c_here = remote(qbuf.at[:, 1 - k], qbuf.at[:, 1 - k], c_send.at[0], c_recv.at[0], partner)
+
+    def c_copy(i):
+        here = qbuf.at[(s + GROUPS - ORDER[i]) % GROUPS, k]
+        return remote(here, here, c_send.at[i], c_recv.at[i], partner)
+
+    def c_landed(i):
+        here = qbuf.at[(s + GROUPS - ORDER[i]) % GROUPS, 1 - k]
+        return remote(here, here, c_send.at[i], c_recv.at[i], partner)
+
     total = GROUPS * CORES * queries
 
-    def widen(g, carry):
-        chunk = queries * CORES * blk
-        own = pl.ds(pl.multiple_of(g * chunk, chunk), chunk)
+    def put_together(i):
+        source = (s + GROUPS - ORDER[i]) % GROUPS
+        lines = queries * blk
         for lanes in range(width // LANES):
-            cols = qbuf[g, :, :, :, lanes * LANES : (lanes + 1) * LANES]
-            qwide[lanes, own, :] = cols.reshape(chunk, LANES).astype(F32)
-        return carry
-
-    def regroup(r, carry):
-        for lanes in range(width // LANES):
-            cols = qwide[lanes, pl.ds(r, total, stride=blk), :]
-            qrow[r, :, lanes * LANES : (lanes + 1) * LANES] = cols.astype(BF16)
-        return carry
+            for core in range(CORES):
+                cols = qbuf[source, core, :, :, lanes * LANES : (lanes + 1) * LANES]
+                qwide[lanes, core * LANES : core * LANES + lines] = cols.reshape(lines, LANES).astype(F32)
+        place = pl.ds(pl.multiple_of(source * blk, blk), blk)
+
+        def one_row(r, carry):
+            for lanes in range(width // LANES):
+                cols = qwide[lanes, pl.ds(r, blk, stride=blk), :]
+                qrow[r, place, lanes * LANES : (lanes + 1) * LANES] = cols.astype(BF16)
+            return carry
+
+        lax.fori_loop(0, blk, one_row, 0)
 
     def score(low, high):
-        padded, step = 16, 4
+        padded, step = 16, 8
 
         def some_rows(g, scores):
             for r in [g * step + n for n in range(step)]:
@@ -238,10 +245,10 @@
                 scores += lax.dot_general(both, qrow[r], NT, preferred_element_type=F32)
             return scores
 
-        scores = lax.fori_loop(0, blk // step, some_rows, jnp.zeros((2 * padded, total), F32))
+        scores = lax.fori_loop(0, blk // step, some_rows, jnp.zeros((2 * padded, LANES), F32))
         scores = scores[:padded] + scores[padded:]
         for i in range(low, high):
-            part[i, :seqs, :total] = scores[(i - low) * seqs : (i - low + 1) * seqs]
+            part[i, :seqs] = scores[(i - low) * seqs : (i - low + 1) * seqs]
 
     me = s * GROUPS + mp
 
@@ -255,7 +262,7 @@
                 if i or o:
                     r_copy(i, (mp + o) % GROUPS).start()
 
-    waited, loaded = set(), set()
+    waited, loaded, begun = set(), set(), set()
 
     def wait(copy, *name):
         if name not in waited:
@@ -265,33 +272,31 @@
     def y_wait(i, second, way):
         wait(lambda *_: y_landed(i, first_col[i] ^ second, way), "y", i, second, way)
 
-    def multiply_half(part_of, source):
-        low, high = (0, SPLIT) if part_of == 0 else (SPLIT, GROUPS)
+    def multiply_half(part_of, source, second):
+        low, high = (0, HALF) if part_of == 0 else (HALF, GROUPS)
         dy = (0, -1, 1, 2)[source]
         for i in range(low, high):
-            if source == 0:
+            if source == 0 and not second:
                 if i:
                     wait(a_landed, "a", i)
+            elif source == 0:
                 wait(z_landed, "z", i)
+            elif second and i in EARLY:
+                e_landed(i, dy).wait_recv()
             elif source == 3:
-                wait(lambda *_: f_landed(i, first_col[i]), "f", i, 0)
-                if i in EARLY:
-                    e_landed(i, 2).wait_recv()
-                else:
-                    wait(lambda *_: f_landed(i, 1 - first_col[i]), "f", i, 1)
+                wait(lambda *_: f_landed(i, first_col[i] ^ second), "f", i, second)
             else:
-                y_wait(i, 0, source - 1)
-                if i in EARLY:
-                    e_landed(i, dy).wait_recv()
-                else:
-                    y_wait(i, 1, source - 1)
-        multiply(dy % YS, low, high, source == 0, dy not in loaded)
-        loaded.add(dy)
-        if source == 3:
-            score(low, high)
-            send_scores(low, high)
+                y_wait(i, second, source - 1)
+        m, name = at(dy % YS, part_of ^ second), (dy, part_of ^ second)
+        if name not in loaded:
+            loaded.add(name)
+            pltpu.make_async_copy(u_hbm.at[m], u_v.at[m], u_sem.at[m]).wait()
+        multiply(m, low, high, part_of not in begun)
+        begun.add(part_of)
 
     for step, *arg in STEPS:
+        if step in "AZFEGQCR":
+            arg = [ORDER.index(arg[0])] + arg[1:]
         if step == "A":
             wait(a_landed, "a", arg[0])
             both_ways(arg[0], first_col[arg[0]])
@@ -314,31 +319,42 @@
         elif step == "Q":
             q_copy(arg[0]).start()
         elif step == "C":
-            for i in range(1, GROUPS):
+            i = arg[0]
+            if i:
                 q_landed(i).wait_recv()
-            q_own.wait()
-            c_copy.start()
+            else:
+                q_own.wait()
+            c_copy(i).start()
         elif step == "R":
-            c_here.wait_recv()
-            lax.fori_loop(0, GROUPS, widen, 0)
-            lax.fori_loop(0, blk, regroup, 0)
+            c_landed(arg[0]).wait_recv()
+            put_together(arg[0])
+        elif step == "M":
+            multiply_half(*arg)
         else:
-            multiply_half(*arg)
+            low, high = (0, HALF) if arg[0] == 0 else (HALF, GROUPS)
+            score(low, high)
+            send_scores(low, high)
 
     got[me] = part[0]
     others = got.at[pl.ds(0, GROUPS * GROUPS - 1)]
     r_all = remote(others, others, r_send.at[0], r_recv.at[0], partner)
     r_all.wait_recv()
     scale = 1.0 / math.sqrt(LEN * rows * width * GROUPS)
-    out_ref[...] = jnp.sum(got[...], axis=0)[:seqs, :total] * scale
+    lines = jnp.concatenate([jnp.sum(got[...], axis=0)] * 2, axis=0)
+    line = lax.broadcasted_iota(jnp.int32, (LANES, total), 0)
+    query = lax.broadcasted_iota(jnp.int32, (LANES, total), 1)
+    wanted = query // queries * 8 + query % queries
+    chosen = jnp.where(line == wanted, 1.0, 0.0).astype(F32)
+    picked = jnp.dot(lines, chosen, precision=lax.Precision.HIGHEST, preferred_element_type=F32)
+    out_ref[...] = picked[:seqs] * scale
 
     r_all.wait_send()
-    c_copy.wait_send()
     for i in range(GROUPS):
         if i:
             a_copy(i).wait_send()
             q_copy(i).wait_send()
         z_copy(i).wait_send()
+        c_copy(i).wait_send()
         if i in EARLY:
             for dy in (1, -1, 2):
                 e_copy(i, dy).wait_send()
@@ -374,8 +390,8 @@
             pltpu.VMEM((GROUPS, piece, width), BF16),
             pltpu.VMEM((GROUPS, GROUPS, piece, width), BF16),
             pltpu.VMEM((GROUPS, CORES, queries, blk, width), BF16),
-            pltpu.VMEM((width // LANES, total * blk, LANES), F32),
-            pltpu.VMEM((blk, total, width), BF16),
+            pltpu.VMEM((width // LANES, CORES * LANES, LANES), F32),
+            pltpu.VMEM((blk, LANES, width), BF16),
             pltpu.VMEM((width // LANES, GROUPS * piece + blk * 4, LANES), F32),
             pltpu.VMEM((GROUPS, 4, LANES), F32),
             pltpu.VMEM((GROUPS * GROUPS, 4, LANES), F32),
@@ -383,7 +399,7 @@
             dma((GROUPS,)), dma((GROUPS,)), dma((GROUPS,)), dma((GROUPS,)),
             dma((len(EARLY), YS)), dma((len(EARLY), YS)),
             dma((2, 2, GROUPS)), dma((2, 2, GROUPS)), dma((2, GROUPS)), dma((2, GROUPS)),
-            dma((GROUPS,)), dma((GROUPS,)), dma((1,)), dma((1,)), dma((1,)), dma((1,)),
+            dma((GROUPS,)), dma((GROUPS,)), dma((GROUPS,)), dma((GROUPS,)), dma((1,)), dma((1,)),
         ],
         compiler_params=pltpu.CompilerParams(
             collective_id=0, has_side_effects=True, vmem_limit_bytes=58 * 2**20

time: 80.5 us -> 78 us (0.969)
  Pallas kernels: 79 us -> 76.6 us
    pallas_call x1, Pallas kernels: 79 us -> 76.6 us  [local(): pl.pallas_call(functools.partial(kernel, dims), out_shape=jax.ShapeDtypeS...]
where the time goes in v4:
time: 78 us; the launch traced here: 77.9 us
  Pallas kernels  76.6 us (98%)
  local copies, waits for them, and re-layouts  1.26 us (2%)
    pallas_call x1, Pallas kernels, local(): pl.pallas_call(functools.partial(kernel, dims), out_shape=jax.ShapeDtypeS...  76.6 us

profile of v4, /device:TPU:0, one launch (start us, length us, event | category | flops | bytes accessed | tf_op | source)
XLA Modules:
  0.0 77.9 jit_solution(5368598870703412188)
XLA Ops:
  0.0 76.6 %shard_map.73 = f32[3,96]{1,0:T(4,128)} custom-call(bf16[64,3072]{1,0:T(8,128)(2,1)} %bitcast.10, s32[3,1,1024]{2,1,0:T(1,128)} %bitcast.11, f32[2,64,64]{2,1,0:T(8,128)} %basis_ref.1, bf16[3,1024,1024]{2,1,0:T(8,128)(2,1)} %bitcast.7, bf16[8,1024,1024]{2,1,0:T(8,128)(2,1)} %bitcast.6, f32[128,1024]{1,0:T(8,128)} %bitcast.9, bf16[6,128,1024]{2,1,0:T(8,128)(2,1)} %bitcast.8), custom_call_target="tpu_custom_call" | custom-call | tf_op jit(solution)/shard_map/pallas_call | solution.py:381
  76.6 1.3 %copy.9 = f32[3,96]{1,0:T(4,128)} copy(f32[3,96]{1,0:T(4,128)} %shard_map.73) | data formatting | bytes 2304

commit v5 on v4

--- a/solution.py
+++ b/solution.py
@@ -27,9 +27,9 @@
     ("F", 4, 0), ("Z", 4), ("M", 1, 0, 0), ("M", 0, 0, 0), ("E", 5, 1), ("F", 5, 0), ("E", 5, 0), ("M", 0, 1, 0),
     ("M", 0, 2, 0), ("G", 2), ("F", 6, 1), ("M", 1, 1, 0), ("M", 1, 2, 0), ("F", 7, 1), ("C", 0), ("C", 1), ("C", 7),
     ("C", 4), ("C", 3), ("C", 5), ("C", 6), ("C", 2), ("M", 1, 0, 1), ("M", 0, 0, 1), ("R", 0), ("R", 1), ("R", 7),
-    ("R", 4), ("F", 3, 1), ("M", 1, 3, 0), ("M", 0, 3, 0), ("R", 3), ("R", 5), ("R", 6), ("R", 2), ("M", 0, 1, 1),
-    ("M", 0, 2, 1), ("G", 5), ("F", 4, 1), ("M", 1, 1, 1), ("M", 1, 2, 1), ("M", 1, 3, 1), ("S", 1), ("M", 0, 3, 1),
-    ("S", 0),
+    ("R", 4), ("F", 3, 1), ("M", 1, 3, 0), ("M", 0, 3, 0), ("R", 3), ("R", 5), ("R", 6), ("R", 2), ("G", 5),
+    ("M", 0, 1, 1), ("M", 0, 2, 1), ("F", 4, 1), ("M", 1, 1, 1), ("M", 1, 2, 1), ("M", 1, 3, 1), ("S", 1),
+    ("M", 0, 3, 1), ("S", 0),
 )
 NT = (((1,), (1,)), ((), ()))
 
@@ -189,7 +189,7 @@
         sequence(n)
         if n == 0:
             pl.semaphore_wait(barrier, len(greeted))
-        for i in range(1, GROUPS):
+        for i in (4, 5, 1, 2, 6, 7, 3):
             a_copy(i, n, n + 1).start()
         gat[mp, 0, n * blk : (n + 1) * blk] = raw[s, n * blk : (n + 1) * blk]
         y_copy(0, first_col[0], 0, n, n + 1).start()

time: 78 us -> 77.7 us (level)
  no operation moved by 1% of the time
where the time goes in v5:
time: 77.7 us; the launch traced here: 77.5 us
  Pallas kernels  76.3 us (98%)
  local copies, waits for them, and re-layouts  1.26 us (2%)
    pallas_call x1, Pallas kernels, local(): pl.pallas_call(functools.partial(kernel, dims), out_shape=jax.ShapeDtypeS...  76.3 us

profile of v5, /device:TPU:0, one launch (start us, length us, event | category | flops | bytes accessed | tf_op | source)
XLA Modules:
  0.0 77.5 jit_solution(6343317214075322183)
XLA Ops:
  0.0 76.3 %shard_map.73 = f32[3,96]{1,0:T(4,128)} custom-call(bf16[64,3072]{1,0:T(8,128)(2,1)} %bitcast.10, s32[3,1,1024]{2,1,0:T(1,128)} %bitcast.11, f32[2,64,64]{2,1,0:T(8,128)} %basis_ref.1, bf16[3,1024,1024]{2,1,0:T(8,128)(2,1)} %bitcast.7, bf16[8,1024,1024]{2,1,0:T(8,128)(2,1)} %bitcast.6, f32[128,1024]{1,0:T(8,128)} %bitcast.9, bf16[6,128,1024]{2,1,0:T(8,128)(2,1)} %bitcast.8), custom_call_target="tpu_custom_call" | custom-call | tf_op jit(solution)/shard_map/pallas_call | solution.py:381
  76.3 1.3 %copy.9 = f32[3,96]{1,0:T(4,128)} copy(f32[3,96]{1,0:T(4,128)} %shard_map.73) | data formatting | bytes 2304

commit v6 on v5

--- a/solution.py
+++ b/solution.py
@@ -199,7 +199,7 @@
     q_own.start()
     for m in range(GROUPS):
         pltpu.make_async_copy(u_hbm.at[m], u_v.at[m], u_sem.at[m]).start()
-    acc[:, GROUPS * piece :] = jnp.zeros((width // LANES, blk * 4, LANES), F32)
+    acc[:, GROUPS * piece :] = jnp.zeros((width // LANES, blk * 5, LANES), F32)
     part[...] = jnp.zeros(part.shape, F32)
     qwide[...] = jnp.zeros(qwide.shape, F32)
     eig_copy.wait()
@@ -390,9 +390,9 @@
             pltpu.VMEM((GROUPS, piece, width), BF16),
             pltpu.VMEM((GROUPS, GROUPS, piece, width), BF16),
             pltpu.VMEM((GROUPS, CORES, queries, blk, width), BF16),
-            pltpu.VMEM((width // LANES, CORES * LANES, LANES), F32),
+            pltpu.VMEM((width // LANES, CORES * LANES + blk, LANES), F32),
             pltpu.VMEM((blk, LANES, width), BF16),
-            pltpu.VMEM((width // LANES, GROUPS * piece + blk * 4, LANES), F32),
+            pltpu.VMEM((width // LANES, GROUPS * piece + blk * 5, LANES), F32),
             pltpu.VMEM((GROUPS, 4, LANES), F32),
             pltpu.VMEM((GROUPS * GROUPS, 4, LANES), F32),
             dma((seqs,)), dma((GROUPS,)), dma((2,)),

time: 77.7 us -> 77.7 us (level)
  no operation moved by 1% of the time
where the time goes in v6:
time: 77.7 us; the launch traced here: 77.5 us
  Pallas kernels  76.3 us (98%)
  local copies, waits for them, and re-layouts  1.26 us (2%)
    pallas_call x1, Pallas kernels, local(): pl.pallas_call(functools.partial(kernel, dims), out_shape=jax.ShapeDtypeS...  76.3 us

profile of v6, /device:TPU:0, one launch (start us, length us, event | category | flops | bytes accessed | tf_op | source)
XLA Modules:
  0.0 77.5 jit_solution(2116379052677538201)
XLA Ops:
  0.0 76.3 %shard_map.73 = f32[3,96]{1,0:T(4,128)} custom-call(bf16[64,3072]{1,0:T(8,128)(2,1)} %bitcast.10, s32[3,1,1024]{2,1,0:T(1,128)} %bitcast.11, f32[2,64,64]{2,1,0:T(8,128)} %basis_ref.1, bf16[3,1024,1024]{2,1,0:T(8,128)(2,1)} %bitcast.7, bf16[8,1024,1024]{2,1,0:T(8,128)(2,1)} %bitcast.6, f32[128,1024]{1,0:T(8,128)} %bitcast.9, bf16[6,128,1024]{2,1,0:T(8,128)(2,1)} %bitcast.8), custom_call_target="tpu_custom_call" | custom-call | tf_op jit(solution)/shard_map/pallas_call | solution.py:381
  76.3 1.3 %copy.9 = f32[3,96]{1,0:T(4,128)} copy(f32[3,96]{1,0:T(4,128)} %shard_map.73) | data formatting | bytes 2304
